TPU v7x, 32 devices: a whole 2x2x4 slice. The times are simulated.
32 devices in a mesh: ka: 16 (over z, y, core), ga: 2 (over x).
Axes of the slice: x: 2, y: 2, z: 4, core: 2. Of those that a mesh axis runs over, the one named last changes fastest.
Arguments:
- pair_density: bfloat16 [64, 64, 1536], P('ka', None, 'ga'), may hold values from -0.15625 to 0.15625
- screened: bfloat16 [3, 1536, 1536], P(None, 'ga'), as said below
- vectors: bfloat16 [64, 64, 128], P('ka'), may hold values from -6 to 6
- energy: float32 [64, 64], P('ka'), may hold values from 1 to 3
- transfer_index: int32 [64, 5, 4], P('ka'), may hold values from 0 to 2, as said below
Outputs:
- image: float32 [64, 64, 128], P('ka')
Inputs may be any that keep to these rules, and one draw needn't show every extreme that they name: `transfer_index`: every value from 0 to 2 may occur; both ends occur; the entry for the pair (k, k2) equals the entry for the pair (k2, k). `screened`: each slice is a symmetric matrix.
All inputs are finite; a program needn't handle non-finite values.
Results may differ from a plain program's by a relative error of at most 0.0019.
Values may be sent and summed in bfloat16 or wider, within the bound.
A program may use at most 64 MiB of HBM per device.

v0:
```python
import jax
import jax.numpy as jnp
from jax import lax
from jax.sharding import PartitionSpec as P


def shifted(value, axis, by):
    length = lax.axis_size(axis)
    return lax.ppermute(value, axis, [(i, (i + by) % length) for i in range(length)])


def kernel_terms(columns, visit_vectors, dens_own, indices, offset):
    partners = jnp.arange(columns.shape[0], dtype=jnp.int32)
    chosen = columns[partners[None, :], indices[:, offset, :]]
    blocks = jnp.einsum("ksg,kjgt->kjst", dens_own, chosen, preferred_element_type=jnp.float32)
    return jnp.einsum(
        "kjst,jtb->ksb", blocks, visit_vectors.astype(jnp.float32), precision=lax.Precision.HIGHEST
    )


def neighbours(travelling):
    return [
        (distance, shifted((travelling[0], travelling[1]), "ka", distance))
        for distance in (1, -1, 2, -2)
    ]


def local(pair_density, screened, vectors, energy, transfer_index):

    def full_product(gathered):
        return jnp.einsum(
            "qgh,jth->jqgt", screened, gathered, preferred_element_type=jnp.float32
        ).astype(jnp.bfloat16)

    gathered = lax.all_gather(pair_density, "ga", axis=2, tiled=True)
    own_columns = full_product(gathered)
    travelling = (gathered, vectors)
    coupled = kernel_terms(own_columns, vectors, pair_density, transfer_index, 2)
    for distance, arrived in neighbours(travelling):
        columns = full_product(arrived[0])
        coupled = coupled + kernel_terms(
            columns, arrived[1], pair_density, transfer_index, 2 - distance
        )
    summed = lax.psum(coupled, "ga")
    return energy[:, :, None] * vectors.astype(jnp.float32) + summed


def solution(mesh):
    return jax.shard_map(
        local,
        mesh=mesh,
        in_specs=(
            P("ka", None, "ga"),
            P(None, "ga", None),
            P("ka", None, None),
            P("ka", None),
            P("ka", None, None),
        ),
        out_specs=P("ka", None, None),
        check_vma=False,
    )
```

profile of v0, /device:TPU:0, one launch (start us, length us, event | category | flops | bytes accessed | tf_op | source)
XLA Modules:
  0.0 135.1 jit_solution(16806393456522183649)
XLA Ops:
  6.5 0.0 all-reduce.2.cloned.1.call-start
  6.5 14.8 %all_gather.3 = bf16[4,64,1536]{2,1,0:T(8,128)(2,1)} all-gather(bf16[4,64,768]{2,1,0:T(8,128)(2,1)} %param.5), channel_id=1, replica_groups=mesh['ka'=16,'ga'=2] {'ga'}, dimensions={2}, use_global_device_ids=true | all-gather | bytes 1179648 | tf_op jit(solution)/shard_map/all_gather | solution.py:35
  21.3 4.6 %collective-permute-start.6 = (bf16[4,64,1536]{2,1,0:T(8,128)(2,1)}, bf16[4,64,1536]{2,1,0:T(8,128)(2,1)}, u32[]{:S(2)}, u32[]{:S(2)}) collective-permute-start(bf16[4,64,1536]{2,1,0:T(8,128)(2,1)} %all_gather.3), channel_id=1, source_target_pairs={{0,28},{2,30},{4,0},{6,2},{8,4},{10,6},{12,8},{14,10},{16,12},{18,... | collective-permute-start | bytes 2359304 | tf_op jit(solution)/shard_map/ppermute | solution.py:9
  25.8 0.0 collective-permute-start.4
  25.9 4.7 %collective-permute-start.7 = (bf16[4,64,128]{2,1,0:T(8,128)(2,1)}, bf16[4,64,128]{2,1,0:T(8,128)(2,1)}, u32[]{:S(2)}, u32[]{:S(2)}) collective-permute-start(bf16[4,64,128]{2,1,0:T(8,128)(2,1)} %param.7), channel_id=1, source_target_pairs={{0,28},{2,30},{4,0},{6,2},{8,4},{10,6},{12,8},{14,10},{16,12},{18,... | collective-permute-start | bytes 196616 | tf_op jit(solution)/shard_map/ppermute | solution.py:9
  30.6 0.0 collective-permute-start.5
  30.6 2.5 %collective-permute-start.2 = (bf16[4,64,1536]{2,1,0:T(8,128)(2,1)}, bf16[4,64,1536]{2,1,0:T(8,128)(2,1)}, u32[]{:S(2)}, u32[]{:S(2)}) collective-permute-start(bf16[4,64,1536]{2,1,0:T(8,128)(2,1)} %all_gather.3), channel_id=1, source_target_pairs={{0,30},{2,0},{4,2},{6,4},{8,6},{10,8},{12,10},{14,12},{16,14},{18,... | collective-permute-start | bytes 2359304 | tf_op jit(solution)/shard_map/ppermute | solution.py:9
  33.1 1.4 %slice_reduce_fusion.3 = (s32[4,4]{1,0:T(4,128)S(1)}, s32[4,4]{1,0:T(4,128)S(1)}, s32[4,4]{1,0:T(4,128)S(1)}, s32[4,4]{1,0:T(4,128)S(1)}, s32[4,4]{1,0:T(4,128)S(1)}) fusion(s32[4,5,4]{1,2,0:T(4,128)} %param.9), kind=kLoop, calls=%fused_computation.58 | loop fusion | bytes 640 | tf_op jit(solution)/shard_map/slice | solution.py:14
  34.5 5.4 %fusion.37 = bf16[4,3,768,64]{2,3,1,0:T(8,128)(2,1)S(1)} fusion(bf16[3,768,1536]{2,1,0:T(8,128)(2,1)} %param.6, bf16[4,64,1536]{2,1,0:T(8,128)(2,1)} %all_gather.3), kind=kOutput, calls=%fused_computation.24 | convolution fusion | flops 1812529152 | bytes 9043968 | tf_op jit(solution)/shard_map/qgh,jth->jqgt/dot_general | solution.py:31
  39.8 0.1 reshape.144
  39.9 0.0 copy-start
  39.9 0.7 gather_fusion
  40.6 0.3 copy-done
  40.9 0.9 convolution_bitcast_fusion.4
  41.8 0.1 reshape.168
  41.9 0.1 reshape.162
  42.0 0.1 reshape.156
  42.1 0.1 reshape.150
  42.1 1.9 %convolution_bitcast_fusion.9 = f32[4,64,128]{2,1,0:T(8,128)} fusion(f32[4,4,64,64]{3,2,1,0:T(8,128)S(1)} %convolution_bitcast_fusion.4, bf16[4,64,128]{2,1,0:T(8,128)(2,1)} %param.7), kind=kOutput, calls=%fused_computation.34 | convolution fusion | flops 100663296 | bytes 458752 | tf_op jit(solution)/shard_map/kjst,jtb->ksb/dot_general | solution.py:16
  44.0 15.3 %collective-permute-done.6 = bf16[4,64,1536]{2,1,0:T(8,128)(2,1)} collective-permute-done((bf16[4,64,1536]{2,1,0:T(8,128)(2,1)}, bf16[4,64,1536]{2,1,0:T(8,128)(2,1)}, u32[]{:S(2)}, u32[]{:S(2)}) %collective-permute-start.6) | collective-permute-done | bytes 786464 | tf_op jit(solution)/shard_map/ppermute | solution.py:9
  59.3 0.0 collective-permute-start.3
  59.3 5.3 %fusion.25 = bf16[4,3,768,64]{2,3,1,0:T(8,128)(2,1)S(1)} fusion(bf16[3,768,1536]{2,1,0:T(8,128)(2,1)} %param.6, bf16[4,64,1536]{2,1,0:T(8,128)(2,1)} %collective-permute-done.6), kind=kOutput, calls=%fused_computation.20 | convolution fusion | flops 1812529152 | bytes 9043968 | tf_op jit(solution)/shard_map/qgh,jth->jqgt/dot_general | solution.py:31
  64.6 0.7 gather_fusion.4
  65.3 2.5 %collective-permute-done.4 = bf16[4,64,1536]{2,1,0:T(8,128)(2,1)} collective-permute-done((bf16[4,64,1536]{2,1,0:T(8,128)(2,1)}, bf16[4,64,1536]{2,1,0:T(8,128)(2,1)}, u32[]{:S(2)}, u32[]{:S(2)}) %collective-permute-start.4) | collective-permute-done | bytes 786464 | tf_op jit(solution)/shard_map/ppermute | solution.py:9
  67.7 0.0 collective-permute-start
  67.8 6.3 %fusion.28 = bf16[4,3,768,64]{2,3,1,0:T(8,128)(2,1)} fusion(bf16[3,768,1536]{2,1,0:T(8,128)(2,1)} %param.6, bf16[4,64,1536]{2,1,0:T(8,128)(2,1)} %collective-permute-done.4), kind=kOutput, calls=%fused_computation.21 | convolution fusion | flops 1812529152 | bytes 9043968 | tf_op jit(solution)/shard_map/qgh,jth->jqgt/dot_general | solution.py:31
  74.0 1.9 %gather_fusion.3 = bf16[16,768,64]{1,2,0:T(8,128)(2,1)S(1)} fusion(bf16[4,3,768,64]{2,3,1,0:T(8,128)(2,1)} %fusion.28, s32[16]{0:T(128)S(1)} %reshape.162), kind=kCustom, calls=%fused_computation.3 | custom fusion | bytes 3145856 | tf_op jit(solution)/shard_map/gather | solution.py:14
  76.0 0.0 collective-permute-done.2
  76.0 2.7 %collective-permute-start.1 = (bf16[4,64,128]{2,1,0:T(8,128)(2,1)}, bf16[4,64,128]{2,1,0:T(8,128)(2,1)}, u32[]{:S(2)}, u32[]{:S(2)}) collective-permute-start(bf16[4,64,128]{2,1,0:T(8,128)(2,1)} %param.7), channel_id=1, source_target_pairs={{0,2},{2,4},{4,6},{6,8},{8,10},{10,12},{12,14},{14,16},{16,18},{18... | collective-permute-start | bytes 196616 | tf_op jit(solution)/shard_map/ppermute | solution.py:9
  78.6 6.3 %fusion.31 = bf16[4,3,768,64]{2,3,1,0:T(8,128)(2,1)} fusion(bf16[3,768,1536]{2,1,0:T(8,128)(2,1)} %param.6, bf16[4,64,1536]{2,1,0:T(8,128)(2,1)} %collective-permute-done.2), kind=kOutput, calls=%fused_computation.22 | convolution fusion | flops 1812529152 | bytes 9043968 | tf_op jit(solution)/shard_map/qgh,jth->jqgt/dot_general | solution.py:31
  85.0 3.1 %gather_fusion.2 = bf16[16,768,64]{1,2,0:T(8,128)(2,1)} fusion(bf16[4,3,768,64]{2,3,1,0:T(8,128)(2,1)} %fusion.31, s32[16]{0:T(128)S(1)} %reshape.156), kind=kCustom, calls=%fused_computation.2 | custom fusion | bytes 3145856 | tf_op jit(solution)/shard_map/gather | solution.py:14
  88.0 1.7 %convolution_bitcast_fusion = f32[4,4,64,64]{3,2,1,0:T(8,128)} fusion(bf16[4,4,768,64]{2,3,1,0:T(8,128)(2,1)S(1)} %bitcast.162, bf16[4,64,768]{2,1,0:T(8,128)(2,1)S(1)} %copy-done), kind=kOutput, calls=%fused_computation.25 | convolution fusion | flops 100663296 | bytes 2228224 | tf_op jit(solution)/shard_map/ksg,kjgt->kjst/dot_general | solution.py:15
  89.7 0.0 copy-start.1
  89.7 1.7 %convolution_bitcast_fusion.1 = f32[4,4,64,64]{3,2,1,0:T(8,128)} fusion(bf16[4,4,768,64]{2,3,1,0:T(8,128)(2,1)S(1)} %bitcast.163, bf16[4,64,768]{2,1,0:T(8,128)(2,1)S(1)} %copy-done), kind=kOutput, calls=%fused_computation.26 | convolution fusion | flops 100663296 | bytes 2228224 | tf_op jit(solution)/shard_map/ksg,kjgt->kjst/dot_general | solution.py:15
  91.4 0.0 copy-done.1
  91.4 1.7 %convolution_bitcast_fusion.2 = f32[4,4,64,64]{3,2,1,0:T(8,128)} fusion(bf16[4,4,768,64]{2,3,1,0:T(8,128)(2,1)S(1)} %bitcast.164, bf16[4,64,768]{2,1,0:T(8,128)(2,1)S(1)} %copy-done), kind=kOutput, calls=%fused_computation.27 | convolution fusion | flops 100663296 | bytes 2228224 | tf_op jit(solution)/shard_map/ksg,kjgt->kjst/dot_general | solution.py:15
  93.0 0.0 collective-permute-done
  93.0 5.3 %fusion.34 = bf16[4,3,768,64]{2,3,1,0:T(8,128)(2,1)S(1)} fusion(bf16[3,768,1536]{2,1,0:T(8,128)(2,1)} %param.6, bf16[4,64,1536]{2,1,0:T(8,128)(2,1)} %collective-permute-done), kind=kOutput, calls=%fused_computation.23 | convolution fusion | flops 1812529152 | bytes 9043968 | tf_op jit(solution)/shard_map/qgh,jth->jqgt/dot_general | solution.py:31
  98.3 0.7 gather_fusion.1
  99.0 0.0 copy-start.4
  99.0 0.0 copy-start.3
  99.0 0.0 copy-start.2
  99.0 0.9 convolution_bitcast_fusion.3
  99.9 0.0 copy-start.5
  99.9 0.0 collective-permute-done.7
  99.9 0.1 copy-done.4
  100.0 1.2 convolution_bitcast_fusion.5
  101.3 0.0 copy-start.6
  101.3 0.0 collective-permute-done.5
  101.3 0.0 copy-done.3
  101.3 1.2 convolution_bitcast_fusion.6
  102.5 0.0 collective-permute-done.3
  102.6 0.0 copy-done.2
  102.6 1.2 convolution_bitcast_fusion.7
  103.8 0.0 collective-permute-done.1
  103.8 0.0 copy-done.5
  103.8 1.9 %fusion.43 = f32[4,64,128]{2,1,0:T(8,128)} fusion(f32[4,64,128]{2,1,0:T(8,128)S(1)} %convolution_bitcast_fusion.5, f32[4,64,128]{2,1,0:T(8,128)S(1)} %convolution_bitcast_fusion.6, f32[4,64,128]{2,1,0:T(8,128)S(1)} %convolution_bitcast_fusion.7, f32[4,64,128]{2,1,0:T(8,128)S(1)} %copy-done.5, f32[4,4,64,64]{3,2,1,0:T(8,128)S(1)} %convolution_bitcast_fusion.3, ...), kind=kOutput, calls=%fused_computation.38 | convolution fusion | flops 100794368 | bytes 983040 | tf_op jit(solution)/shard_map/kjst,jtb->ksb/dot_general | solution.py:16
  105.7 0.0 all-reduce.2.cloned.1.call-update
  105.7 20.9 %all-reduce.2.cloned.1.call-done = f32[4,64,128]{2,1,0:T(8,128)} async-done(((f32[4,64,128]{2,1,0:T(8,128)}), f32[4,64,128]{2,1,0:T(8,128)}) %all-reduce.2.cloned.1.call-update) | async-done | bytes 131088 | tf_op jit(solution)/shard_map/psum | solution.py:44
  126.6 0.0 copy-done.6
  126.6 1.7 %multiply_add_fusion = f32[4,64,128]{2,1,0:T(8,128)} fusion(f32[4,64,128]{2,1,0:T(8,128)} %all-reduce.2.cloned.1.call-done, bf16[4,64,128]{2,1,0:T(8,128)(2,1)} %param.7, f32[4,64]{1,0:T(4,128)S(1)} %copy-done.6), kind=kLoop, calls=%fused_computation.49 | loop fusion | flops 98304 | bytes 328704 | tf_op jit(solution)/shard_map/add | solution.py:45
  (5 shorter events, 0.0 us)
Async XLA Ops:
  6.5 120.1 %all-reduce.2.cloned.1.call-start = ((), (), s32[]{:S(2)}) async-start(), calls=%async_computation | async-start | bytes 262144 | tf_op jit(solution)/shard_map/psum | solution.py:44
  21.3 38.0 %collective-permute-start.6 = (bf16[4,64,1536]{2,1,0:T(8,128)(2,1)}, bf16[4,64,1536]{2,1,0:T(8,128)(2,1)}, u32[]{:S(2)}, u32[]{:S(2)}) collective-permute-start(bf16[4,64,1536]{2,1,0:T(8,128)(2,1)} %all_gather.3), channel_id=1, source_target_pairs={{0,28},{2,30},{4,0},{6,2},{8,4},{10,6},{12,8},{14,10},{16,12},{18,... | collective-permute-start | bytes 2359304 | tf_op jit(solution)/shard_map/ppermute | solution.py:9
  25.8 41.9 %collective-permute-start.4 = (bf16[4,64,1536]{2,1,0:T(8,128)(2,1)}, bf16[4,64,1536]{2,1,0:T(8,128)(2,1)}, u32[]{:S(2)}, u32[]{:S(2)}) collective-permute-start(bf16[4,64,1536]{2,1,0:T(8,128)(2,1)} %all_gather.3), channel_id=1, source_target_pairs={{0,4},{2,6},{4,8},{6,10},{8,12},{10,14},{12,16},{14,18},{16,20},{1... | collective-permute-start | bytes 2359304 | tf_op jit(solution)/shard_map/ppermute | solution.py:9
  25.9 74.0 %collective-permute-start.7 = (bf16[4,64,128]{2,1,0:T(8,128)(2,1)}, bf16[4,64,128]{2,1,0:T(8,128)(2,1)}, u32[]{:S(2)}, u32[]{:S(2)}) collective-permute-start(bf16[4,64,128]{2,1,0:T(8,128)(2,1)} %param.7), channel_id=1, source_target_pairs={{0,28},{2,30},{4,0},{6,2},{8,4},{10,6},{12,8},{14,10},{16,12},{18,... | collective-permute-start | bytes 196616 | tf_op jit(solution)/shard_map/ppermute | solution.py:9
  30.6 70.7 %collective-permute-start.5 = (bf16[4,64,128]{2,1,0:T(8,128)(2,1)}, bf16[4,64,128]{2,1,0:T(8,128)(2,1)}, u32[]{:S(2)}, u32[]{:S(2)}) collective-permute-start(bf16[4,64,128]{2,1,0:T(8,128)(2,1)} %param.7), channel_id=1, source_target_pairs={{0,4},{2,6},{4,8},{6,10},{8,12},{10,14},{12,16},{14,18},{16,20},{1... | collective-permute-start | bytes 196616 | tf_op jit(solution)/shard_map/ppermute | solution.py:9
  30.6 45.4 %collective-permute-start.2 = (bf16[4,64,1536]{2,1,0:T(8,128)(2,1)}, bf16[4,64,1536]{2,1,0:T(8,128)(2,1)}, u32[]{:S(2)}, u32[]{:S(2)}) collective-permute-start(bf16[4,64,1536]{2,1,0:T(8,128)(2,1)} %all_gather.3), channel_id=1, source_target_pairs={{0,30},{2,0},{4,2},{6,4},{8,6},{10,8},{12,10},{14,12},{16,14},{18,... | collective-permute-start | bytes 2359304 | tf_op jit(solution)/shard_map/ppermute | solution.py:9
  39.9 1.0 copy-start
  59.3 43.3 %collective-permute-start.3 = (bf16[4,64,128]{2,1,0:T(8,128)(2,1)}, bf16[4,64,128]{2,1,0:T(8,128)(2,1)}, u32[]{:S(2)}, u32[]{:S(2)}) collective-permute-start(bf16[4,64,128]{2,1,0:T(8,128)(2,1)} %param.7), channel_id=1, source_target_pairs={{0,30},{2,0},{4,2},{6,4},{8,6},{10,8},{12,10},{14,12},{16,14},{18,... | collective-permute-start | bytes 196616 | tf_op jit(solution)/shard_map/ppermute | solution.py:9
  67.7 25.3 %collective-permute-start = (bf16[4,64,1536]{2,1,0:T(8,128)(2,1)}, bf16[4,64,1536]{2,1,0:T(8,128)(2,1)}, u32[]{:S(2)}, u32[]{:S(2)}) collective-permute-start(bf16[4,64,1536]{2,1,0:T(8,128)(2,1)} %all_gather.3), channel_id=1, source_target_pairs={{0,2},{2,4},{4,6},{6,8},{8,10},{10,12},{12,14},{14,16},{16,18},{18... | collective-permute-start | bytes 2359304 | tf_op jit(solution)/shard_map/ppermute | solution.py:9
  76.0 27.8 %collective-permute-start.1 = (bf16[4,64,128]{2,1,0:T(8,128)(2,1)}, bf16[4,64,128]{2,1,0:T(8,128)(2,1)}, u32[]{:S(2)}, u32[]{:S(2)}) collective-permute-start(bf16[4,64,128]{2,1,0:T(8,128)(2,1)} %param.7), channel_id=1, source_target_pairs={{0,2},{2,4},{4,6},{6,8},{8,10},{10,12},{12,14},{14,16},{16,18},{18... | collective-permute-start | bytes 196616 | tf_op jit(solution)/shard_map/ppermute | solution.py:9
  89.7 1.7 %copy-start.1 = (bf16[16,768,64]{1,2,0:T(8,128)(2,1)S(1)}, bf16[16,768,64]{1,2,0:T(8,128)(2,1)}, u32[]{:S(2)}) copy-start(bf16[16,768,64]{1,2,0:T(8,128)(2,1)} %gather_fusion.2) | copy-start | bytes 4718596
  99.0 1.0 copy-start.4
  99.0 2.3 %copy-start.3 = (f32[4,4,64,64]{3,2,1,0:T(8,128)S(1)}, f32[4,4,64,64]{3,2,1,0:T(8,128)}, u32[]{:S(2)}) copy-start(f32[4,4,64,64]{3,2,1,0:T(8,128)} %convolution_bitcast_fusion.1) | copy-start | bytes 786436
  99.0 3.5 %copy-start.2 = (f32[4,4,64,64]{3,2,1,0:T(8,128)S(1)}, f32[4,4,64,64]{3,2,1,0:T(8,128)}, u32[]{:S(2)}) copy-start(f32[4,4,64,64]{3,2,1,0:T(8,128)} %convolution_bitcast_fusion.2) | copy-start | bytes 786436
  99.9 3.9 %copy-start.5 = (f32[4,64,128]{2,1,0:T(8,128)S(1)}, f32[4,64,128]{2,1,0:T(8,128)}, u32[]{:S(2)}) copy-start(f32[4,64,128]{2,1,0:T(8,128)} %convolution_bitcast_fusion.9) | copy-start | bytes 393220
  101.3 25.3 %copy-start.6 = (f32[4,64]{1,0:T(4,128)S(1)}, f32[4,64]{1,0:T(4,128)}, u32[]{:S(2)}) copy-start(f32[4,64]{1,0:T(4,128)} %param.8) | copy-start | bytes 3076
Sparse Core Ops, SparseCore 0:
  105.9 20.7 all-reduce.1
where the time goes:
time: 136 us; the launch traced here: 135 us
  matrix products  42.7 us (31%)
  waiting for transfers between devices  38.7 us (28%)
  blocking collectives  14.8 us (11%)
  starting transfers between devices  14.4 us (11%)
  between operations  13.6 us (10%)
  local copies, waits for them, and re-layouts  9.21 us (7%)
  other arithmetic  1.71 us (1%)
    dot_general x5, matrix products, full_product(): jnp.einsum('qgh,jth->jqgt', screened, gathered, preferred_element_type=jn...  28.5 us
    psum x1, waiting for transfers between devices, local(): summed = lax.psum(coupled, 'ga')  20.9 us
    ppermute x8, waiting for transfers between devices, shifted(): lax.ppermute(value, axis, [(i, (i + by) % length) for i in range(length)])  17.8 us
    all_gather x1, blocking collectives, local(): gathered = lax.all_gather(pair_density, 'ga', axis=2, tiled=True)  14.8 us
    ppermute x8, starting transfers between devices, shifted(): lax.ppermute(value, axis, [(i, (i + by) % length) for i in range(length)])  14.4 us
    dot_general x5, matrix products, kernel_terms(): jnp.einsum('kjst,jtb->ksb', blocks, visit_vectors.astype(jnp.float32), pr...  7.48 us
    gather x5, local copies, waits for them, and re-layouts, kernel_terms(): chosen = columns[partners[None, :], indices[:, offset, :]]  6.95 us
    dot_general x5, matrix products, kernel_terms(): jnp.einsum('ksg,kjgt->kjst', dens_own, chosen, preferred_element_type=jnp...  6.72 us
  transfers between devices with their start and end apart: 9, of which 3 were waited for; matrix products, arithmetic and copies ran while one was open for 37% of the time, Pallas kernels for 0%

commit v1 on v0

v1 whole, which is shorter than its diff:
```python
import functools

import jax
import jax.numpy as jnp
from jax import lax
from jax.experimental import pallas as pl
from jax.experimental.pallas import tpu as pltpu
from jax.sharding import PartitionSpec as P

MESH = pl.DeviceIdType.MESH
NT = (((1,), (1,)), ((), ()))
TN = (((0,), (0,)), ((), ()))
PIECES = 3


def shifted(value, axis, by):
    length = lax.axis_size(axis)
    return lax.ppermute(value, axis, [(i, (i + by) % length) for i in range(length)])


def general(pair_density, screened, vectors, energy, transfer_index):
    count = screened.shape[0]
    gathered = lax.all_gather(pair_density, "ga", axis=2, tiled=True)
    own = jnp.einsum(
        "qgh,ksh->kqsg", screened, gathered, preferred_element_type=jnp.float32
    ).astype(jnp.bfloat16)
    coupled = 0.0
    for distance in (0, 1, -1, 2, -2):
        dens, vecs = pair_density, vectors
        if distance:
            dens, vecs = shifted((dens, vecs), "ka", distance)
        every = jnp.einsum("kqsg,jtg->kqsjt", own, dens, preferred_element_type=jnp.float32)
        picks = transfer_index[:, 2 - distance, :][:, None, :, None]
        blocks = every[:, 0]
        for q in range(1, count):
            blocks = jnp.where(picks == q, every[:, q], blocks)
        coupled = coupled + jnp.einsum(
            "ksjt,jtb->ksb", blocks, vecs.astype(jnp.float32), precision=lax.Precision.HIGHEST
        )
    summed = lax.psum(coupled, "ga")
    return energy[:, :, None] * vectors.astype(jnp.float32) + summed


def pair_kernel(
    n, nq, k_dev, states,
    x_hbm, v_hbm, idx_hbm, e_hbm, w_hbm, out,
    x, v, idx, e, wv, xo, x2, v2, x3, v3, racc, r, c1s, c1r, c2s, c2r, ts, tr,
    wsem, gs, gr, ss, sr,
):
    me = lax.axis_index("ka")
    gx = lax.axis_index("ga")
    odd = lax.rem(me, 2)
    rows, gl = x.shape
    small = [
        pltpu.make_async_copy(src, dst, wsem.at[nq + i])
        for i, (src, dst) in enumerate(((x_hbm, x), (v_hbm, v), (idx_hbm, idx), (e_hbm, e)))
    ]
    for load in small:
        load.start()

    def at(by):
        return lax.rem(me + by + n, n)

    def to(ka, ga=gx):
        return {"ka": ka, "ga": ga}

    def remote(src, dst, s, where):
        return pltpu.make_async_remote_copy(
            src_ref=src, dst_ref=dst, send_sem=ss.at[s], recv_sem=sr.at[s],
            device_id=where, device_id_type=MESH,
        )

    loads = [pltpu.make_async_copy(w_hbm.at[q], wv.at[q], wsem.at[q]) for q in range(nq)]
    for load in loads:
        load.start()

    barrier = pltpu.get_barrier_semaphore()
    for by in (-2, -1, 1, 2):
        pl.semaphore_signal(barrier, inc=1, device_id=to(at(by)), device_id_type=MESH)
    pl.semaphore_signal(barrier, inc=1, device_id=to(me, 1 - gx), device_id_type=MESH)
    pl.semaphore_wait(barrier, 5)

    piece = gl // PIECES
    gathers = []
    for c in range(PIECES):
        cols = pl.ds(c * piece, piece)
        gathers.append(
            pltpu.make_async_remote_copy(
                src_ref=x_hbm.at[:, cols], dst_ref=xo.at[:, cols],
                send_sem=gs.at[c], recv_sem=gr.at[c],
                device_id=to(me, 1 - gx), device_id_type=MESH,
            )
        )
    across = to(at(4 * odd - 2))
    core = to(at(1 - 2 * odd))

    def parts(src, dst, first, where):
        return [
            remote(
                src.at[:, pl.ds(c * piece, piece)], dst.at[:, pl.ds(c * piece, piece)],
                first + c, where,
            )
            for c in range(PIECES)
        ]

    far = parts(x_hbm, x2, 0, across)
    far_v = remote(v_hbm, v2, PIECES, across)
    near_odd = parts(x_hbm, x3, PIECES + 1, core)
    near_even = parts(x2, x3, PIECES + 1, core)
    near_odd_v = remote(v_hbm, v3, 2 * PIECES + 1, core)
    near_even_v = remote(v2, v3, 2 * PIECES + 1, core)
    last = 2 * PIECES + 2

    for c in range(PIECES):
        gathers[c].start()
        far[c].start()
    far_v.start()

    @pl.when(odd == 1)
    def _():
        for copy in near_odd + [near_odd_v]:
            copy.start()

    own_at = pl.multiple_of(gx * gl, 128)
    other_at = pl.multiple_of((1 - gx) * gl, 128)

    for load in small:
        load.wait()
    one = lax.broadcasted_iota(jnp.int32, (states, states), 0)
    one = one == lax.broadcasted_iota(jnp.int32, (states, states), 1)
    for k in range(k_dev):
        at_k = slice(k * states, (k + 1) * states)
        column = jnp.sum(jnp.where(one, e[k:k + 1, :], 0.0), axis=1, keepdims=True)
        out[at_k] = column * v[at_k].astype(jnp.float32)
    for q in range(nq):
        loads[q].wait()
        racc[q] = lax.dot_general(
            wv[q, :, pl.ds(own_at, gl)], x[...], NT, preferred_element_type=jnp.float32
        )

    for c in range(PIECES):
        gathers[c].wait_recv()
        cols = pl.ds(pl.multiple_of(other_at + c * piece, 128), piece)
        for q in range(nq):
            new = racc[q] + lax.dot_general(
                wv[q, :, cols], xo[:, c * piece:(c + 1) * piece], NT,
                preferred_element_type=jnp.float32,
            )
            if c < PIECES - 1:
                racc[q] = new
            else:
                r[q] = new.astype(jnp.bfloat16)
        far[c].wait_recv()

        @pl.when(odd == 0)
        def _(c=c):
            near_even[c].start()

    far_v.wait_recv()

    @pl.when(odd == 0)
    def _():
        near_even_v.start()

    lane = lax.broadcasted_iota(jnp.int32, (states, rows), 1) // states

    def kernel_of(dens, table):
        every = [
            jnp.dot(dens[...], r[q], preferred_element_type=jnp.float32) for q in range(nq)
        ]
        strips = []
        for j in range(k_dev):
            at_j = slice(j * states, (j + 1) * states)
            pick = jnp.zeros((states, rows), jnp.int32)
            for k in range(k_dev):
                pick = jnp.where(lane == k, table[k:k + 1, j:j + 1], pick)
            strip = every[0][at_j]
            for q in range(1, nq):
                strip = jnp.where(pick == q, every[q][at_j], strip)
            strips.append(strip)
        block = jnp.concatenate(strips, axis=0)
        high = block.astype(jnp.bfloat16)
        return high, (block - high.astype(jnp.float32)).astype(jnp.bfloat16)

    def forth(pair, vecs):
        return sum(jnp.dot(p, vecs[...], preferred_element_type=jnp.float32) for p in pair)

    def back(pair, vecs):
        return sum(
            lax.dot_general(p, vecs[...], TN, preferred_element_type=jnp.float32) for p in pair
        )

    pair1 = kernel_of(x2, jnp.where(odd == 1, idx[:, :, 0], idx[:, :, 4]))
    c1s[...] = forth(pair1, v).astype(jnp.bfloat16)
    back1 = remote(c1s, c1r, last, to(at(2 - 4 * odd)))
    back1.start()

    for copy in near_odd + [near_odd_v]:
        copy.wait_recv()
    pair2 = kernel_of(x3, idx[:, :, 3])
    c2s[...] = forth(pair2, v).astype(jnp.bfloat16)
    back2 = remote(c2s, c2r, last + 1, to(at(1)))
    back2.start()

    total = back(pair1, v2) + back(pair2, v3) + forth(kernel_of(x, idx[:, :, 2]), v)
    back1.wait_recv()
    back2.wait_recv()
    total += c1r[...].astype(jnp.float32) + c2r[...].astype(jnp.float32)
    ts[...] = total.astype(jnp.bfloat16)
    swap = remote(ts, tr, last + 2, to(me, 1 - gx))
    swap.start()
    for copy in gathers + far + near_odd + [far_v, near_odd_v, back1, back2]:
        copy.wait_send()
    swap.wait()
    out[...] += ts[...].astype(jnp.float32) + tr[...].astype(jnp.float32)


def local(pair_density, screened, vectors, energy, transfer_index):
    n = lax.axis_size("ka")
    k_dev, states, gl = pair_density.shape
    nq, _, ng = screened.shape
    width = vectors.shape[2]
    fits = gl % (128 * PIECES) == 0 and states % 16 == 0 and width % 128 == 0
    if lax.axis_size("ga") != 2 or n < 6 or n % 2 or not fits:
        return general(pair_density, screened, vectors, energy, transfer_index)
    rows = k_dev * states
    half = jnp.bfloat16
    hbm = pl.BlockSpec(memory_space=pl.ANY)
    image = pl.pallas_call(
        functools.partial(pair_kernel, n, nq, k_dev, states),
        out_shape=jax.ShapeDtypeStruct((rows, width), jnp.float32),
        in_specs=[hbm] * 5,
        out_specs=pl.BlockSpec(memory_space=pltpu.VMEM),
        scratch_shapes=[
            pltpu.VMEM((rows, gl), half),
            pltpu.VMEM((rows, width), half),
            pltpu.VMEM((k_dev, k_dev, 5), jnp.int32),
            pltpu.VMEM((k_dev, states), jnp.float32),
            pltpu.VMEM((nq, gl, ng), half),
            pltpu.VMEM((rows, gl), half),
            pltpu.VMEM((rows, gl), half),
            pltpu.VMEM((rows, width), half),
            pltpu.VMEM((rows, gl), half),
            pltpu.VMEM((rows, width), half),
            pltpu.VMEM((nq, gl, rows), jnp.float32),
            pltpu.VMEM((nq, gl, rows), half),
        ]
        + [pltpu.VMEM((rows, width), half)] * 6
        + [
            pltpu.SemaphoreType.DMA((nq + 4,)),
            pltpu.SemaphoreType.DMA((PIECES,)),
            pltpu.SemaphoreType.DMA((PIECES,)),
            pltpu.SemaphoreType.DMA((2 * PIECES + 5,)),
            pltpu.SemaphoreType.DMA((2 * PIECES + 5,)),
        ],
        compiler_params=pltpu.CompilerParams(
            collective_id=0, has_side_effects=True, vmem_limit_bytes=63 * 1024 * 1024 + 512 * 1024
        ),
        cost_estimate=pl.CostEstimate(
            flops=2 * nq * gl * rows * (ng + 3 * rows),
            bytes_accessed=2 * nq * gl * ng, transcendentals=0,
        ),
    )(
        pair_density.reshape(rows, gl), vectors.reshape(rows, width),
        jnp.swapaxes(transfer_index, 1, 2), energy, screened
    )
    return image.reshape(k_dev, states, width)


def solution(mesh):
    return jax.shard_map(
        local,
        mesh=mesh,
        in_specs=(
            P("ka", None, "ga"),
            P(None, "ga", None),
            P("ka", None, None),
            P("ka", None),
            P("ka", None, None),
        ),
        out_specs=P("ka", None, None),
        check_vma=False,
    )
```

time: 136 us -> 28.9 us (0.21)
  matrix products: 42.7 us -> 0 us
  waiting for transfers between devices: 38.7 us -> 0 us
  Pallas kernels: 0 us -> 27.1 us
  blocking collectives: 14.8 us -> 0 us
  starting transfers between devices: 14.4 us -> 0 us
  between operations: 13.6 us -> 0.01 us
  local copies, waits for them, and re-layouts: 9.21 us -> 1.57 us
  other arithmetic: 1.71 us -> 0 us
    dot_general x15 -> x0, matrix products: 42.7 us -> none  [the longest x5 28.5 us: full_product(): jnp.einsum('qgh,jth->jqgt', screened, gathered, preferred_element_type=jn...]
    pallas_call x0 -> x1, Pallas kernels: none -> 27.1 us  [local(): pl.pallas_call(functools.partial(pair_kernel, n, nq, k_dev, states), out_...]
    psum x1 -> x0, waiting for transfers between devices: 20.9 us -> none  [local(): summed = lax.psum(coupled, 'ga')]
    ppermute x8 -> x0, waiting for transfers between devices: 17.8 us -> none  [shifted(): lax.ppermute(value, axis, [(i, (i + by) % length) for i in range(length)])]
    all_gather x1 -> x0, blocking collectives: 14.8 us -> none  [local(): gathered = lax.all_gather(pair_density, 'ga', axis=2, tiled=True)]
    ppermute x8 -> x0, starting transfers between devices: 14.4 us -> none  [shifted(): lax.ppermute(value, axis, [(i, (i + by) % length) for i in range(length)])]
    gather x5 -> x0, local copies, waits for them, and re-layouts: 6.95 us -> none  [kernel_terms(): chosen = columns[partners[None, :], indices[:, offset, :]]]
    add x1 -> x0, other arithmetic: 1.66 us -> none  [local(): return energy[:, :, None] * vectors.astype(jnp.float32) + summed]
  transfers between devices with their start and end apart: 9 -> 0, of which waited for: 3 -> 0; matrix products, arithmetic and copies ran while one was open for 37% -> 0% of each run, Pallas kernels for 0% -> 0%
where the time goes in v1:
time: 28.9 us; the launch traced here: 28.7 us
  Pallas kernels  27.1 us (94%)
  local copies, waits for them, and re-layouts  1.57 us (5%)
    pallas_call x1, Pallas kernels, local(): pl.pallas_call(functools.partial(pair_kernel, n, nq, k_dev, states), out_...  27.1 us
    unnamed x1, local copies, waits for them, and re-layouts  1.57 us

profile of v1, /device:TPU:0, one launch (start us, length us, event | category | flops | bytes accessed | tf_op | source)
XLA Modules:
  0.0 28.7 jit_solution(10685271418935634084)
XLA Ops:
  0.0 27.1 %shard_map.55 = f32[256,128]{1,0:T(8,128)} custom-call(bf16[256,768]{1,0:T(8,128)(2,1)} %bitcast.5, bf16[256,128]{1,0:T(8,128)(2,1)} %bitcast.6, s32[4,4,5]{2,1,0:T(4,128)} %bitcast.7, f32[4,64]{1,0:T(4,128)} %e_hbm.1, bf16[3,768,1536]{2,1,0:T(8,128)(2,1)} %w_hbm.1), custom_call_target="tpu_custom_call" | custom-call | flops 2717908992 | bytes 7077888 | tf_op jit(solution)/shard_map/pallas_call | solution.py:229
  27.1 1.6 %copy.7 = f32[4,64,128]{2,1,0:T(8,128)} copy(f32[4,64,128]{2,1,0:T(8,128)} %bitcast.4) | data formatting | bytes 262144

commit v2 on v1

--- a/solution.py
+++ b/solution.py
@@ -44,7 +44,7 @@
 def pair_kernel(
     n, nq, k_dev, states,
     x_hbm, v_hbm, idx_hbm, e_hbm, w_hbm, out,
-    x, v, idx, e, wv, xo, x2, v2, x3, v3, racc, r, c1s, c1r, c2s, c2r, ts, tr,
+    x, v, idx, e, wv, xo, x2, v2, x3, v3, racc, r, c1s, c1r, c1x, c2s, c2r, c2x, ts, tr,
     wsem, gs, gr, ss, sr,
 ):
     me = lax.axis_index("ka")
@@ -77,8 +77,9 @@
     barrier = pltpu.get_barrier_semaphore()
     for by in (-2, -1, 1, 2):
         pl.semaphore_signal(barrier, inc=1, device_id=to(at(by)), device_id_type=MESH)
-    pl.semaphore_signal(barrier, inc=1, device_id=to(me, 1 - gx), device_id_type=MESH)
-    pl.semaphore_wait(barrier, 5)
+    for by in (-2, -1, 0, 1, 2):
+        pl.semaphore_signal(barrier, inc=1, device_id=to(at(by), 1 - gx), device_id_type=MESH)
+    pl.semaphore_wait(barrier, 9)
 
     piece = gl // PIECES
     gathers = []
@@ -194,23 +195,31 @@
     c1s[...] = forth(pair1, v).astype(jnp.bfloat16)
     back1 = remote(c1s, c1r, last, to(at(2 - 4 * odd)))
     back1.start()
-
+    cross1 = remote(c1s, c1x, last + 4, to(at(2 - 4 * odd), 1 - gx))
+    cross1.start()
+
+    total = back(pair1, v2) + forth(kernel_of(x, idx[:, :, 2]), v)
     for copy in near_odd + [near_odd_v]:
         copy.wait_recv()
     pair2 = kernel_of(x3, idx[:, :, 3])
     c2s[...] = forth(pair2, v).astype(jnp.bfloat16)
     back2 = remote(c2s, c2r, last + 1, to(at(1)))
     back2.start()
-
-    total = back(pair1, v2) + back(pair2, v3) + forth(kernel_of(x, idx[:, :, 2]), v)
-    back1.wait_recv()
-    back2.wait_recv()
-    total += c1r[...].astype(jnp.float32) + c2r[...].astype(jnp.float32)
+    cross2 = remote(c2s, c2x, last + 3, to(at(1), 1 - gx))
+    cross2.start()
+
+    total += back(pair2, v3)
     ts[...] = total.astype(jnp.bfloat16)
     swap = remote(ts, tr, last + 2, to(me, 1 - gx))
     swap.start()
-    for copy in gathers + far + near_odd + [far_v, near_odd_v, back1, back2]:
+    for copy in gathers + far + near_odd + [far_v, near_odd_v, back1, back2, cross1, cross2]:
         copy.wait_send()
+    back1.wait_recv()
+    cross1.wait_recv()
+    out[...] += c1r[...].astype(jnp.float32) + c1x[...].astype(jnp.float32)
+    back2.wait_recv()
+    cross2.wait_recv()
+    out[...] += c2r[...].astype(jnp.float32) + c2x[...].astype(jnp.float32)
     swap.wait()
     out[...] += ts[...].astype(jnp.float32) + tr[...].astype(jnp.float32)
 
@@ -245,13 +254,13 @@
             pltpu.VMEM((nq, gl, rows), jnp.float32),
             pltpu.VMEM((nq, gl, rows), half),
         ]
-        + [pltpu.VMEM((rows, width), half)] * 6
+        + [pltpu.VMEM((rows, width), half)] * 8
         + [
             pltpu.SemaphoreType.DMA((nq + 4,)),
             pltpu.SemaphoreType.DMA((PIECES,)),
             pltpu.SemaphoreType.DMA((PIECES,)),
-            pltpu.SemaphoreType.DMA((2 * PIECES + 5,)),
-            pltpu.SemaphoreType.DMA((2 * PIECES + 5,)),
+            pltpu.SemaphoreType.DMA((2 * PIECES + 7,)),
+            pltpu.SemaphoreType.DMA((2 * PIECES + 7,)),
         ],
         compiler_params=pltpu.CompilerParams(
             collective_id=0, has_side_effects=True, vmem_limit_bytes=63 * 1024 * 1024 + 512 * 1024

time: 28.9 us -> 27.6 us (0.955)
  Pallas kernels: 27.1 us -> 25.8 us
    pallas_call x1, Pallas kernels: 27.1 us -> 25.8 us  [local(): pl.pallas_call(functools.partial(pair_kernel, n, nq, k_dev, states), out_...]
where the time goes in v2:
time: 27.6 us; the launch traced here: 27.4 us
  Pallas kernels  25.8 us (93%)
  local copies, waits for them, and re-layouts  1.57 us (6%)
    pallas_call x1, Pallas kernels, local(): pl.pallas_call(functools.partial(pair_kernel, n, nq, k_dev, states), out_...  25.8 us
    unnamed x1, local copies, waits for them, and re-layouts  1.57 us

profile of v2, /device:TPU:0, one launch (start us, length us, event | category | flops | bytes accessed | tf_op | source)
XLA Modules:
  0.0 27.4 jit_solution(10850582874196544628)
XLA Ops:
  0.0 25.8 %shard_map.55 = f32[256,128]{1,0:T(8,128)} custom-call(bf16[256,768]{1,0:T(8,128)(2,1)} %bitcast.5, bf16[256,128]{1,0:T(8,128)(2,1)} %bitcast.6, s32[4,4,5]{2,1,0:T(4,128)} %bitcast.7, f32[4,64]{1,0:T(4,128)} %e_hbm.1, bf16[3,768,1536]{2,1,0:T(8,128)(2,1)} %w_hbm.1), custom_call_target="tpu_custom_call" | custom-call | flops 2717908992 | bytes 7077888 | tf_op jit(solution)/shard_map/pallas_call | solution.py:238
  25.8 1.6 %copy.7 = f32[4,64,128]{2,1,0:T(8,128)} copy(f32[4,64,128]{2,1,0:T(8,128)} %bitcast.4) | data formatting | bytes 262144
